TPU v7x, 32 devices: a whole 2x2x4 slice. The times are simulated.
32 devices in a mesh: dp: 4 (over z), ctx: 2 (over core), tensor: 4 (over y, x).
Axes of the slice: x: 2, y: 2, z: 4, core: 2. Of those that a mesh axis runs over, the one named last changes fastest.
Arguments:
- tokens: bfloat16 [4, 4096, 1024], P('dp', ('ctx', 'tensor')), may hold values from -6 to 6
- gain: bfloat16 [2, 1024], P(None, ('dp', 'ctx')), may hold values from 0.5 to 1.5
- w_z: bfloat16 [2, 1024, 2048], P(None, ('dp', 'ctx'), 'tensor'), may hold values from -0.1875 to 0.1875
- w_x: bfloat16 [2, 1024, 2048], P(None, ('dp', 'ctx'), 'tensor'), may hold values from -0.1875 to 0.1875
- w_bc: bfloat16 [2, 1024, 256], P(None, ('dp', 'ctx')), may hold values from -0.1875 to 0.1875
- w_dt: bfloat16 [2, 1024, 32], P(None, ('dp', 'ctx')), may hold values from -0.1875 to 0.1875
- conv_w: bfloat16 [2, 4, 2304], P(None, None, ('dp', 'ctx')), may hold values from -3 to 3
- conv_b: bfloat16 [2, 2304], P(None, ('dp', 'ctx')), may hold values from -0.5 to 0.5
- dt_bias: bfloat16 [2, 32], P(None, ('dp', 'ctx')), may hold values from -6 to -2
- a_log: bfloat16 [2, 32], P(None, ('dp', 'ctx')), may hold values from 0 to 2.5
- d_skip: bfloat16 [2, 32], P(None, ('dp', 'ctx')), may hold values from 0.5 to 1.5
- norm_w: bfloat16 [2, 2048], P(None, ('dp', 'ctx')), may hold values from 0.5 to 1.5
- w_out: bfloat16 [2, 2048, 1024], P(None, 'tensor', ('dp', 'ctx')), may hold values from -0.125 to 0.125
- cotangent: bfloat16 [4, 4096, 1024], P('dp', ('ctx', 'tensor')), may hold values from -6 to 6
Outputs:
- outputs: bfloat16 [4, 4096, 1024], P('dp', ('ctx', 'tensor'))
- grad_tokens: float32 [4, 4096, 1024], P('dp', ('ctx', 'tensor'))
- grad_gain: float32 [2, 1024], P(None, ('dp', 'ctx'))
- grad_w_z: float32 [2, 1024, 2048], P(None, ('dp', 'ctx'), 'tensor')
- grad_w_x: float32 [2, 1024, 2048], P(None, ('dp', 'ctx'), 'tensor')
- grad_w_bc: float32 [2, 1024, 256], P(None, ('dp', 'ctx'))
- grad_w_dt: float32 [2, 1024, 32], P(None, ('dp', 'ctx'))
- grad_conv_w: float32 [2, 4, 2304], P(None, None, ('dp', 'ctx'))
- grad_conv_b: float32 [2, 2304], P(None, ('dp', 'ctx'))
- grad_dt_bias: float32 [2, 32], P(None, ('dp', 'ctx'))
- grad_a_log: float32 [2, 32], P(None, ('dp', 'ctx'))
- grad_d_skip: float32 [2, 32], P(None, ('dp', 'ctx'))
- grad_norm_w: float32 [2, 2048], P(None, ('dp', 'ctx'))
- grad_w_out: float32 [2, 2048, 1024], P(None, 'tensor', ('dp', 'ctx'))
All inputs are finite; a program needn't handle non-finite values.
Results may differ from a plain program's by a relative error of at most 0.03.
Values may be sent and summed in bfloat16 or wider, within the bound.
A program may use at most 256 MiB of HBM per device.

v0:
```python
import jax
import jax.numpy as jnp
from jax import lax
from jax.sharding import PartitionSpec as P

NH = 32
HEADDIM = 64
NSTATE = 128
KCONV = 4
SPAN = 256
LAYERS = 2
INNER = 2048


EPS = 1e-05
HIGH = lax.Precision.HIGHEST


def from_behind(array, axis, by):
    peers = lax.axis_size(axis)
    pairs = [(i, i + by) for i in range(peers) if 0 <= i + by < peers]
    return lax.ppermute(array, axis, pairs)


def prefix_2(array, axis, combine, identity):
    peers, mine = (lax.axis_size(axis), lax.axis_index(axis))
    everything = jax.tree.map(
        lambda part, kind: lax.all_gather(part.astype(kind), axis),
        array,
        (jnp.bfloat16, jnp.bfloat16),
    )
    start = jax.tree.map(
        lambda part, zero: jnp.broadcast_to(jnp.asarray(zero, part.dtype), part.shape),
        array,
        identity,
    )

    def prefix_hop(k, before):
        reached = k < mine
        new = combine(
            before, jax.tree.map(lambda part, own: part[k].astype(own.dtype), everything, array)
        )
        return jax.tree.map(lambda a, b: jnp.where(reached, a, b), new, before)

    return lax.fori_loop(0, peers, prefix_hop, start)


def entering(array, axis, combine, identity):
    peers, mine = (lax.axis_size(axis), lax.axis_index(axis))
    everything = jax.tree.map(
        lambda part, kind: lax.all_gather(part.astype(kind), axis),
        array,
        jax.tree.map(lambda a: jnp.bfloat16 if a.dtype == jnp.float32 else a.dtype, array),
    )
    start = jax.tree.map(
        lambda part, zero: jnp.broadcast_to(jnp.asarray(zero, part.dtype), part.shape),
        array,
        identity,
    )

    def entering_hop(k, before):
        at = peers - 1 - k
        reached = at > mine
        new = combine(
            before, jax.tree.map(lambda part, own: part[at].astype(own.dtype), everything, array)
        )
        return jax.tree.map(lambda a, b: jnp.where(reached, a, b), new, before)

    return lax.fori_loop(0, peers, entering_hop, start)


def ssd_block(state_in, inputs):
    head_x, proj_b, proj_c, delta_t, log_decay = inputs
    running = jnp.cumsum(log_decay, axis=0)
    positions = jnp.arange(head_x.shape[0])
    causal = (positions[:, None] >= positions[None, :])[:, :, None]
    spread = running[:, None, :] - running[None, :, :]
    kernel = jnp.where(causal, jnp.exp(jnp.where(causal, spread, 0.0)), 0.0)
    scores = jnp.dot(proj_c, proj_b.T, precision=HIGH, preferred_element_type=jnp.float32)
    mixing = scores[:, :, None] * kernel * delta_t[None, :, :]
    inside = jnp.einsum("tsh,shp->thp", mixing, head_x, precision=HIGH)
    carried = (
        jnp.einsum("tn,hpn->thp", proj_c, state_in, precision=HIGH) * jnp.exp(running)[:, :, None]
    )
    tail_weight = jnp.exp(running[-1][None, :] - running) * delta_t
    update = jnp.einsum("sh,sn,shp->hpn", tail_weight, proj_b, head_x, precision=HIGH)
    new_state = state_in * jnp.exp(running[-1])[:, None, None] + update
    return (new_state, inside + carried)


def scan_blocks(head_x, proj_b, proj_c, delta_t, log_decay):
    token_count = head_x.shape[0]
    block_count = token_count // SPAN
    pieces = (
        head_x.reshape(block_count, SPAN, head_x.shape[1], head_x.shape[2]),
        proj_b.reshape(block_count, SPAN, proj_b.shape[1]),
        proj_c.reshape(block_count, SPAN, proj_c.shape[1]),
        delta_t.reshape(block_count, SPAN, delta_t.shape[1]),
        log_decay.reshape(block_count, SPAN, log_decay.shape[1]),
    )
    zero_state = jnp.zeros((head_x.shape[1], head_x.shape[2], proj_b.shape[1]), jnp.float32)
    final_state, outputs = lax.scan(jax.checkpoint(ssd_block), zero_state, pieces)
    return (final_state, outputs.reshape(head_x.shape))


def inject(proj_c, log_decay, state_in):
    running = jnp.cumsum(log_decay, axis=0)
    return (
        jnp.einsum("tn,hpn->thp", proj_c, state_in, precision=HIGH) * jnp.exp(running)[:, :, None]
    )


def chain_join(earlier, latter):
    return (earlier[0] + latter[0], latter[1] + jnp.exp(latter[0])[:, None, None] * earlier[1])


def silu_grad(values):
    sigmoid_v = jax.nn.sigmoid(values)
    return sigmoid_v * (1.0 + values * (1.0 - sigmoid_v))


def own_slice(vector, start, count):
    return lax.dynamic_slice_in_dim(vector, start, count, 0).astype(jnp.float32)


def place_into(width, piece, start):
    return lax.dynamic_update_slice_in_dim(
        jnp.zeros((width,) + piece.shape[1:], jnp.float32), piece, start, 0
    )


def contract_rows(left, right):
    return lax.dot_general(
        left, right, (((0,), (0,)), ((), ())), preferred_element_type=jnp.float32
    )


def contract_cols(left, right):
    return lax.dot_general(
        left, right, (((1,), (1,)), ((), ())), preferred_element_type=jnp.float32
    )


def fetch_layer(weight_stack, layer_index):
    pieces = tuple((weight[layer_index] for weight in weight_stack))
    return (
        lax.all_gather(pieces[0], ("dp", "ctx"), axis=0, tiled=True),
        lax.all_gather(pieces[1], ("dp", "ctx"), axis=0, tiled=True),
        lax.all_gather(pieces[2], ("dp", "ctx"), axis=0, tiled=True),
        lax.all_gather(pieces[3], ("dp", "ctx"), axis=0, tiled=True),
        lax.all_gather(pieces[4], ("dp", "ctx"), axis=0, tiled=True),
        lax.all_gather(pieces[5], ("dp", "ctx"), axis=1, tiled=True),
        lax.all_gather(pieces[6], ("dp", "ctx"), axis=0, tiled=True),
        lax.all_gather(pieces[7], ("dp", "ctx"), axis=0, tiled=True),
        lax.all_gather(pieces[8], ("dp", "ctx"), axis=0, tiled=True),
        lax.all_gather(pieces[9], ("dp", "ctx"), axis=0, tiled=True),
        lax.all_gather(pieces[10], ("dp", "ctx"), axis=0, tiled=True),
        lax.all_gather(pieces[11], ("dp", "ctx"), axis=1, tiled=True),
    )


def reduce_grads(parts):
    summed = (
        lax.psum_scatter(
            parts[0].astype(jnp.bfloat16), ("dp", "ctx"), scatter_dimension=0, tiled=True
        ).astype(jnp.float32),
        lax.psum_scatter(
            parts[1].astype(jnp.bfloat16), ("dp", "ctx"), scatter_dimension=0, tiled=True
        ).astype(jnp.float32),
        lax.psum_scatter(
            parts[2].astype(jnp.bfloat16), ("dp", "ctx"), scatter_dimension=0, tiled=True
        ).astype(jnp.float32),
        lax.psum_scatter(
            parts[3].astype(jnp.bfloat16), ("dp", "ctx"), scatter_dimension=0, tiled=True
        ).astype(jnp.float32),
        lax.psum_scatter(
            parts[4].astype(jnp.bfloat16), ("dp", "ctx"), scatter_dimension=0, tiled=True
        ).astype(jnp.float32),
        lax.psum_scatter(
            parts[5].astype(jnp.bfloat16), ("dp", "ctx"), scatter_dimension=1, tiled=True
        ).astype(jnp.float32),
        lax.psum_scatter(
            parts[6].astype(jnp.bfloat16), ("dp", "ctx"), scatter_dimension=0, tiled=True
        ).astype(jnp.float32),
        lax.psum_scatter(
            parts[7].astype(jnp.bfloat16), ("dp", "ctx"), scatter_dimension=0, tiled=True
        ).astype(jnp.float32),
        lax.psum_scatter(
            parts[8].astype(jnp.bfloat16), ("dp", "ctx"), scatter_dimension=0, tiled=True
        ).astype(jnp.float32),
        lax.psum_scatter(
            parts[9].astype(jnp.bfloat16), ("dp", "ctx"), scatter_dimension=0, tiled=True
        ).astype(jnp.float32),
        lax.psum_scatter(
            parts[10].astype(jnp.bfloat16), ("dp", "ctx"), scatter_dimension=0, tiled=True
        ).astype(jnp.float32),
        lax.psum_scatter(
            parts[11].astype(jnp.bfloat16), ("dp", "ctx"), scatter_dimension=1, tiled=True
        ).astype(jnp.float32),
    )
    shared = (
        lax.psum(summed[0].astype(jnp.bfloat16), "tensor").astype(jnp.float32),
        lax.psum(summed[3].astype(jnp.bfloat16), "tensor").astype(jnp.float32),
        lax.psum(summed[4].astype(jnp.bfloat16), "tensor").astype(jnp.float32),
        lax.psum(summed[5].astype(jnp.bfloat16), "tensor").astype(jnp.float32),
        lax.psum(summed[6].astype(jnp.bfloat16), "tensor").astype(jnp.float32),
        lax.psum(summed[7].astype(jnp.bfloat16), "tensor").astype(jnp.float32),
        lax.psum(summed[8].astype(jnp.bfloat16), "tensor").astype(jnp.float32),
        lax.psum(summed[9].astype(jnp.bfloat16), "tensor").astype(jnp.float32),
        lax.psum(summed[10].astype(jnp.bfloat16), "tensor").astype(jnp.float32),
    )
    return (
        shared[0],
        summed[1],
        summed[2],
        shared[1],
        shared[2],
        shared[3],
        shared[4],
        shared[5],
        shared[6],
        shared[7],
        shared[8],
        summed[11],
    )


def layer_forward(residual, gathered, tensor_at, inner_loc, heads_loc):
    gain, w_z, w_x, w_bc, w_dt, conv_w, conv_b, dt_bias, a_log, d_skip, norm_w, w_out = gathered
    head_start = tensor_at * heads_loc
    chan_start = tensor_at * inner_loc
    inv_rms = lax.rsqrt(jnp.mean(residual * residual, axis=-1, keepdims=True) + EPS)
    normed = (residual * inv_rms * gain.astype(jnp.float32)).astype(jnp.bfloat16)
    rows_all = lax.all_gather(normed, "tensor", axis=0, tiled=True)
    w_main = jnp.concatenate([w_z, w_x, w_bc], axis=1)
    proj_all = jnp.dot(rows_all, w_main, preferred_element_type=jnp.float32)
    w_dt_own = lax.dynamic_slice_in_dim(w_dt, head_start, heads_loc, 1)
    dt_raw = jnp.dot(rows_all, w_dt_own, preferred_element_type=jnp.float32)
    gate_part = proj_all[:, :inner_loc]
    conv_in = proj_all[:, inner_loc:].astype(jnp.bfloat16)
    length = conv_in.shape[0]
    edge_rows = from_behind(conv_in[length - (KCONV - 1) :], "ctx", 1)
    conv_w_own = jnp.concatenate(
        [lax.dynamic_slice_in_dim(conv_w, chan_start, inner_loc, 1), conv_w[:, INNER:]], axis=1
    ).astype(jnp.float32)
    conv_b_own = jnp.concatenate(
        [lax.dynamic_slice_in_dim(conv_b, chan_start, inner_loc, 0), conv_b[INNER:]], axis=0
    ).astype(jnp.float32)
    padded = jnp.concatenate([edge_rows, conv_in], axis=0).astype(jnp.float32)
    conv_out = conv_b_own + sum(
        (conv_w_own[offset] * padded[offset : offset + length] for offset in range(KCONV))
    )
    activated = lax.optimization_barrier(jax.nn.silu(conv_out).astype(jnp.bfloat16)).astype(
        jnp.float32
    )
    head_x = activated[:, :inner_loc].reshape(length, heads_loc, HEADDIM)
    proj_b = activated[:, inner_loc : inner_loc + NSTATE]
    proj_c = activated[:, inner_loc + NSTATE :]
    dt_pre = dt_raw + own_slice(dt_bias, head_start, heads_loc)
    delta_t = jax.nn.softplus(dt_pre)
    decay_rate = -jnp.exp(own_slice(a_log, head_start, heads_loc))
    log_decay = decay_rate * delta_t
    local_state, local_out = scan_blocks(head_x, proj_b, proj_c, delta_t, log_decay)
    total_decay = jnp.sum(log_decay, axis=0)
    prefix = prefix_2(
        (total_decay, local_state),
        "ctx",
        chain_join,
        (jnp.zeros_like(total_decay), jnp.zeros_like(local_state)),
    )
    state_in = prefix[1]
    skip_own = own_slice(d_skip, head_start, heads_loc)
    scanned = local_out + inject(proj_c, log_decay, state_in) + skip_own[None, :, None] * head_x
    gated_y = scanned.reshape(length, inner_loc) * jax.nn.silu(gate_part)
    squares_loc = jnp.sum(gated_y * gated_y, axis=-1)
    norm_own = own_slice(norm_w, chan_start, inner_loc)
    branch = (gated_y * norm_own).astype(jnp.bfloat16)
    partial_out = jnp.dot(branch, w_out, preferred_element_type=jnp.float32)
    out_own, squares_own = (
        lax.psum_scatter(
            partial_out.astype(jnp.bfloat16), "tensor", scatter_dimension=0, tiled=True
        ).astype(jnp.float32),
        lax.psum_scatter(
            squares_loc.astype(jnp.bfloat16), "tensor", scatter_dimension=0, tiled=True
        ).astype(jnp.float32),
    )
    norm_scale = lax.rsqrt(squares_own / INNER + EPS)
    new_resid = residual + norm_scale[:, None] * out_own
    saved_vals = (
        residual,
        inv_rms,
        rows_all,
        w_main,
        gate_part,
        conv_w_own,
        padded,
        conv_out,
        head_x,
        proj_b,
        proj_c,
        dt_pre,
        delta_t,
        decay_rate,
        log_decay,
        state_in,
        total_decay,
        scanned,
        gated_y,
        branch,
        out_own,
        norm_scale,
        w_dt_own,
        skip_own,
        norm_own,
    )
    return (new_resid, saved_vals)


def layer_backward(grad_own, gathered, saved_vals, tensor_at, inner_loc, heads_loc):
    gain, w_z, w_x, w_bc, w_dt, conv_w, conv_b, dt_bias, a_log, d_skip, norm_w, w_out = gathered
    (
        residual,
        inv_rms,
        rows_all,
        w_main,
        gate_part,
        conv_w_own,
        padded,
        conv_out,
        head_x,
        proj_b,
        proj_c,
        dt_pre,
        delta_t,
        decay_rate,
        log_decay,
        state_in,
        total_decay,
        scanned,
        gated_y,
        branch,
        out_own,
        norm_scale,
        w_dt_own,
        skip_own,
        norm_own,
    ) = saved_vals
    head_start = tensor_at * heads_loc
    chan_start = tensor_at * inner_loc
    length = rows_all.shape[0]
    grad_scaled = (norm_scale[:, None] * grad_own).astype(jnp.bfloat16)
    grad_scale = jnp.sum(grad_own * out_own, axis=-1)
    grad_rows = lax.all_gather(grad_scaled, "tensor", axis=0, tiled=True)
    grad_scale_all, scale_all = (
        lax.all_gather(grad_scale, "tensor", axis=0, tiled=True),
        lax.all_gather(norm_scale, "tensor", axis=0, tiled=True),
    )
    grad_wout = contract_rows(branch, grad_rows)
    grad_branch = contract_cols(grad_rows, w_out)
    grad_normw = jnp.sum(grad_branch * gated_y, axis=0)
    grad_gated = grad_branch * norm_own - (grad_scale_all * scale_all**3 / INNER)[:, None] * gated_y
    grad_scan = (grad_gated * jax.nn.silu(gate_part)).reshape(length, heads_loc, HEADDIM)
    grad_gate = grad_gated * scanned.reshape(length, inner_loc) * silu_grad(gate_part)
    grad_skip = jnp.sum(grad_scan * head_x, axis=(0, 2))
    inject_out, inject_pull = jax.vjp(inject, proj_c, log_decay, state_in)
    grad_pc_in, grad_decay_in, grad_state_in = inject_pull(grad_scan)
    suffix = entering(
        (total_decay, grad_state_in),
        "ctx",
        chain_join,
        (jnp.zeros_like(total_decay), jnp.zeros_like(grad_state_in)),
    )
    grad_local_state = suffix[1]
    grad_total = jnp.sum(
        grad_local_state * jnp.exp(total_decay)[:, None, None] * state_in, axis=(1, 2)
    )
    local_vals, local_pull = jax.vjp(scan_blocks, head_x, proj_b, proj_c, delta_t, log_decay)
    grad_hx, grad_pb, grad_pc, grad_dt, grad_decay = local_pull((grad_local_state, grad_scan))
    grad_decay_all = grad_decay + grad_decay_in + grad_total[None, :]
    grad_delta = grad_dt + grad_decay_all * decay_rate
    grad_alog = jnp.sum(grad_decay_all * delta_t, axis=0) * decay_rate
    grad_pre = grad_delta * jax.nn.sigmoid(dt_pre)
    grad_dtbias = jnp.sum(grad_pre, axis=0)
    grad_pre_low = grad_pre.astype(jnp.bfloat16)
    grad_act = jnp.concatenate(
        [
            (grad_hx + grad_scan * skip_own[None, :, None]).reshape(length, inner_loc),
            grad_pb,
            grad_pc + grad_pc_in,
        ],
        axis=1,
    )
    grad_conv = grad_act * silu_grad(conv_out)
    grad_convb = jnp.sum(grad_conv, axis=0)
    grad_convw = jnp.stack(
        [jnp.sum(grad_conv * padded[offset : offset + length], axis=0) for offset in range(KCONV)]
    )
    grad_padded = sum(
        (
            jnp.pad(conv_w_own[offset][None, :] * grad_conv, ((offset, KCONV - 1 - offset), (0, 0)))
            for offset in range(KCONV)
        )
    )
    back_edge = from_behind(grad_padded[: KCONV - 1], "ctx", -1)
    grad_convin = grad_padded[KCONV - 1 :]
    grad_convin = jnp.concatenate(
        [grad_convin[: length - (KCONV - 1)], grad_convin[length - (KCONV - 1) :] + back_edge],
        axis=0,
    )
    grad_proj = jnp.concatenate([grad_gate, grad_convin], axis=1).astype(jnp.bfloat16)
    grad_wmain = contract_rows(rows_all, grad_proj)
    grad_wdt_own = contract_rows(rows_all, grad_pre_low)
    grad_rows_in = contract_cols(grad_proj, w_main) + contract_cols(grad_pre_low, w_dt_own)
    grad_normed = lax.psum_scatter(
        grad_rows_in.astype(jnp.bfloat16), "tensor", scatter_dimension=0, tiled=True
    ).astype(jnp.float32)
    unit_rows = residual * inv_rms
    grad_unit = grad_normed * gain.astype(jnp.float32)
    grad_gain = jnp.sum(grad_normed * unit_rows, axis=0)
    grad_prev = grad_own + inv_rms * (
        grad_unit - unit_rows * jnp.mean(grad_unit * unit_rows, axis=-1, keepdims=True)
    )
    grad_wdt = place_into(NH, grad_wdt_own.T, head_start).T
    conv_x_part = place_into(INNER, grad_convw[:, :inner_loc].T, chan_start).T
    grad_convw_all = jnp.concatenate([conv_x_part, grad_convw[:, inner_loc:]], axis=1)
    grad_convb_all = jnp.concatenate(
        [place_into(INNER, grad_convb[:inner_loc], chan_start), grad_convb[inner_loc:]], axis=0
    )
    parts = (
        grad_gain,
        grad_wmain[:, :inner_loc],
        grad_wmain[:, inner_loc : 2 * inner_loc],
        grad_wmain[:, 2 * inner_loc :],
        grad_wdt,
        grad_convw_all,
        grad_convb_all,
        place_into(NH, grad_dtbias, head_start),
        place_into(NH, grad_alog, head_start),
        place_into(NH, grad_skip, head_start),
        place_into(INNER, grad_normw, chan_start),
        grad_wout,
    )
    return (grad_prev, parts)


def per_device(
    tokens,
    gain,
    w_z,
    w_x,
    w_bc,
    w_dt,
    conv_w,
    conv_b,
    dt_bias,
    a_log,
    d_skip,
    norm_w,
    w_out,
    cotangent,
):
    weight_stack = (
        gain,
        w_z,
        w_x,
        w_bc,
        w_dt,
        conv_w,
        conv_b,
        dt_bias,
        a_log,
        d_skip,
        norm_w,
        w_out,
    )
    tensor_at = lax.axis_index("tensor")
    groups = lax.axis_size("tensor")
    inner_loc = INNER // groups
    heads_loc = NH // groups
    residual = tokens[0].astype(jnp.float32)
    saved_list = []
    fetched = []
    for layer_index in range(LAYERS):
        gathered = fetch_layer(weight_stack, layer_index)
        residual, saved_vals = layer_forward(residual, gathered, tensor_at, inner_loc, heads_loc)
        saved_list.append(saved_vals)
        fetched.append(gathered)
    result = residual.astype(jnp.bfloat16)[None]
    grad_own = cotangent[0].astype(jnp.float32)
    collected = []
    for layer_index in reversed(range(LAYERS)):
        grad_own, parts = layer_backward(
            grad_own, fetched[layer_index], saved_list[layer_index], tensor_at, inner_loc, heads_loc
        )
        collected.insert(0, reduce_grads(parts))
    stacked = tuple(
        (jnp.stack([layer_grads[member] for layer_grads in collected]) for member in range(12))
    )
    return (
        result,
        grad_own[None],
        stacked[0],
        stacked[1],
        stacked[2],
        stacked[3],
        stacked[4],
        stacked[5],
        stacked[6],
        stacked[7],
        stacked[8],
        stacked[9],
        stacked[10],
        stacked[11],
    )


def solution(mesh):
    placed = (
        P("dp", ("ctx", "tensor"), None),
        P(None, ("dp", "ctx")),
        P(None, ("dp", "ctx"), "tensor"),
        P(None, ("dp", "ctx"), "tensor"),
        P(None, ("dp", "ctx"), None),
        P(None, ("dp", "ctx"), None),
        P(None, None, ("dp", "ctx")),
        P(None, ("dp", "ctx")),
        P(None, ("dp", "ctx")),
        P(None, ("dp", "ctx")),
        P(None, ("dp", "ctx")),
        P(None, ("dp", "ctx")),
        P(None, "tensor", ("dp", "ctx")),
        P("dp", ("ctx", "tensor"), None),
    )
    return jax.shard_map(
        per_device,
        mesh=mesh,
        in_specs=placed,
        out_specs=(
            P("dp", ("ctx", "tensor"), None),
            P("dp", ("ctx", "tensor"), None),
            P(None, ("dp", "ctx")),
            P(None, ("dp", "ctx"), "tensor"),
            P(None, ("dp", "ctx"), "tensor"),
            P(None, ("dp", "ctx"), None),
            P(None, ("dp", "ctx"), None),
            P(None, None, ("dp", "ctx")),
            P(None, ("dp", "ctx")),
            P(None, ("dp", "ctx")),
            P(None, ("dp", "ctx")),
            P(None, ("dp", "ctx")),
            P(None, ("dp", "ctx")),
            P(None, "tensor", ("dp", "ctx")),
        ),
        check_vma=False,
    )
```

profile of v0, /device:TPU:0, one launch (start us, length us, event | category | flops | bytes accessed | tf_op | source)
XLA Modules:
  0.0 2225.5 jit_solution(13890112937726430446)
XLA Ops:
  34.9 26.8 %all-reduce.37 = (bf16[2304]{0:T(1024)(128)(2,1)S(1)}, bf16[32]{0:T(256)(128)(2,1)S(1)}, bf16[32]{0:T(256)(128)(2,1)S(1)}, bf16[32]{0:T(256)(128)(2,1)S(1)}, bf1...) all-reduce(bf16[2304]{0:T(1024)(128)(2,1)S(1)} %dynamic-update-slic, ...), channel_id=6, replica_groups=mesh['dp'=4,'ctx'=2,'tensor'=4] {'dp','ctx'}, use_global_device_ids=true, to_apply=%add.14 | all-reduce | flops 4800 | bytes 19200
  78.9 17.5 all-gather.5
  194.4 206.8 %while.162 = (s32[]{:T(128)}, f32[8,64,128]{2,1,0:T(8,128)S(1)}, f32[8,256,8,64]{1,0,3,2:T(8,128)}, f32[8,256,8]{1,2,0:T(8,128)S(1)}, f32[8,256,8]{1,2,0:T(8,128...) while((s32[]{:T(128)}, f32[8,64,128]{2,1,0:T(8,128)S(1)}, ...), condition=%wide.region_4.5_spmd.clone, body=%wide.region_1.4_spmd.clone.sunk | while | flops 909578240 | bytes 6819784 | solution.py:102
  463.1 29.5 %reduce-scatter.29.cloned.1.call-done = bf16[512,1024]{1,0:T(8,128)(2,1)} async-done(((bf16[2048,1024]{1,0:T(8,128)(2,1)}), bf16[512,1024]{1,0:T(8,128)(2,1)}) %reduce-scatter.29.cloned.1.call-update) | async-done | bytes 1048592 | tf_op jit(solution)/shard_map/reduce_scatter | solution.py:280
  543.2 55.0 %all-gather.47.cloned.1.call-done = bf16[2048,1024]{1,0:T(8,128)(2,1)} async-done(((bf16[512,1024]{1,0:T(8,128)(2,1)}), bf16[2048,1024]{1,0:T(8,128)(2,1)}) %all-gather.47.cloned.1.call-update) | async-done | bytes 4194320 | tf_op jit(solution)/shard_map/all_gather | solution.py:234
  648.9 206.5 %while.164 = (s32[]{:T(128)}, f32[8,64,128]{2,1,0:T(8,128)S(1)}, f32[8,256,8,64]{1,0,3,2:T(8,128)}, f32[8,256,8]{1,2,0:T(8,128)}, f32[8,256,8]{1,2,0:T(8,128)}, ...) while((s32[]{:T(128)}, f32[8,64,128]{2,1,0:T(8,128)S(1)}, ...), condition=%wide.region_17.18_spmd.clone, body=%wide.region_14.17_spmd.clone.sunk | while | flops 909578240 | bytes 6819628 | solution.py:102
  914.4 32.0 %reduce-scatter.31.cloned.1.call-done = bf16[512,1024]{1,0:T(8,128)(2,1)} async-done(((bf16[2048,1024]{1,0:T(8,128)(2,1)}), bf16[512,1024]{1,0:T(8,128)(2,1)}) %reduce-scatter.31.cloned.1.call-update) | async-done | bytes 1048592 | tf_op jit(solution)/shard_map/reduce_scatter | solution.py:280
  951.1 40.0 %while.167 = (s32[]{:T(128)}, f32[8,64,128]{2,1,0:T(8,128)S(1)}, f32[8,8,64,128]{3,2,1,0:T(8,128)}, f32[8,256,8]{1,2,0:T(8,128)}, f32[8,256,8]{1,2,0:T(8,128)}, ...) while((s32[]{:T(128)}, f32[8,64,128]{2,1,0:T(8,128)S(1)}, ...), condition=%wide.region_32.33_spmd.clone, body=%wide.region_29.32_spmd.clone.sunk | while | flops 201986080 | bytes 1788192 | solution.py:102
  1045.5 170.6 %while.160 = (s32[]{:T(128)}, f32[8,64,128]{2,1,0:T(8,128)S(1)}, f32[8,256,8,64]{1,3,2,0:T(8,128)}, f32[8,256,128]{2,1,0:T(8,128)}, f32[8,256,128]{2,1,0:T(8,128...) while((s32[]{:T(128)}, f32[8,64,128]{2,1,0:T(8,128)S(1)}, ...), condition=%wide.region_45.46_spmd, body=%wide.region_33.45_spmd.sunk | while | flops 2126469120 | bytes 14830685 | solution.py:102
  1304.0 52.1 %reduce-scatter.33.cloned.1.call-done = bf16[512,1024]{1,0:T(8,128)(2,1)} async-done(((bf16[2048,1024]{1,0:T(8,128)(2,1)}), bf16[512,1024]{1,0:T(8,128)(2,1)}) %reduce-scatter.33.cloned.1.call-update) | async-done | bytes 1048592 | tf_op jit(solution)/shard_map/reduce_scatter | solution.py:414
  1364.7 40.1 %while.169 = (s32[]{:T(128)}, f32[8,64,128]{2,1,0:T(8,128)S(1)}, f32[8,8,64,128]{3,2,1,0:T(8,128)}, f32[8,256,8]{1,2,0:T(8,128)}, f32[8,256,8]{1,2,0:T(8,128)}, ...) while((s32[]{:T(128)}, f32[8,64,128]{2,1,0:T(8,128)S(1)}, ...), condition=%wide.region_58.59_spmd.clone, body=%wide.region_55.58_spmd.clone.sunk | while | flops 201986080 | bytes 1788192 | solution.py:102
  1478.1 170.6 %while.161 = (s32[]{:T(128)}, f32[8,64,128]{2,1,0:T(8,128)S(1)}, f32[8,256,8,64]{1,3,2,0:T(8,128)}, f32[8,256,128]{2,1,0:T(8,128)}, f32[8,256,128]{2,1,0:T(8,128...) while((s32[]{:T(128)}, f32[8,64,128]{2,1,0:T(8,128)S(1)}, ...), condition=%wide.region_71.72_spmd, body=%wide.region_59.71_spmd.sunk | while | flops 2126469120 | bytes 14830685 | solution.py:102
  1777.9 27.0 %reduce-scatter.51.cloned.1.call-done = bf16[128,32]{1,0:T(8,128)(2,1)} async-done(((bf16[1024,32]{1,0:T(8,128)(2,1)}), bf16[128,32]{1,0:T(8,128)(2,1)}) %reduce-scatter.51.cloned.1.call-update) | async-done | bytes 8208
  1805.8 31.6 %reduce-scatter.59.cloned.1.call-done = bf16[128,512]{1,0:T(8,128)(2,1)} async-done(((bf16[1024,512]{1,0:T(8,128)(2,1)}), bf16[128,512]{1,0:T(8,128)(2,1)}) %reduce-scatter.59.cloned.1.call-update) | async-done | bytes 131088
  1839.8 29.5 %reduce-scatter.53.cloned.1.call-done = bf16[288,4]{1,0:T(8,128)(2,1)} async-done(((bf16[2304,4]{1,0:T(8,128)(2,1)}), bf16[288,4]{1,0:T(8,128)(2,1)}) %reduce-scatter.53.cloned.1.call-update) | async-done | bytes 2320
  1870.2 29.8 %reduce-scatter.49.cloned.1.call-done = bf16[128,32]{1,0:T(8,128)(2,1)} async-done(((bf16[1024,32]{1,0:T(8,128)(2,1)}), bf16[128,32]{1,0:T(8,128)(2,1)}) %reduce-scatter.49.cloned.1.call-update) | async-done | bytes 8208
  1900.8 42.6 %all-reduce.42.cloned.1.call-done = (bf16[1,128,256]{2,1,0:T(8,128)(2,1)}, bf16[1,128,256]{2,1,0:T(8,128)(2,1)}) async-done(((bf16[1,128,256]{2,1,0:T(8,128)(2,1)}, bf16[1,128,256]{2,1,0:T(8,128)(2,1)}), (bf16[1,128,256]{2,1,0:T(8,128)(2,1)}, bf16[1,128,256]{2,1,0:T(8,128)(2,1)})) %all-reduce.42.cloned.1.call-update) | async-done | bytes 131088 | tf_op jit(solution)/shard_map/psum | solution.py:203
  1945.0 33.1 %reduce-scatter.57.cloned.1.call-done = bf16[128,512]{1,0:T(8,128)(2,1)} async-done(((bf16[1024,512]{1,0:T(8,128)(2,1)}), bf16[128,512]{1,0:T(8,128)(2,1)}) %reduce-scatter.57.cloned.1.call-update) | async-done | bytes 131088
  1979.9 31.0 %reduce-scatter.43.cloned.1.call-done = bf16[128,512]{1,0:T(8,128)(2,1)} async-done(((bf16[1024,512]{1,0:T(8,128)(2,1)}), bf16[128,512]{1,0:T(8,128)(2,1)}) %reduce-scatter.43.cloned.1.call-update) | async-done | bytes 131088 | tf_op jit(solution)/shard_map/reduce_scatter | solution.py:170
  2010.9 32.8 %reduce-scatter.41.cloned.1.call-done = bf16[128,512]{1,0:T(8,128)(2,1)} async-done(((bf16[1024,512]{1,0:T(8,128)(2,1)}), bf16[128,512]{1,0:T(8,128)(2,1)}) %reduce-scatter.41.cloned.1.call-update) | async-done | bytes 131088 | tf_op jit(solution)/shard_map/reduce_scatter | solution.py:170
  2045.5 31.2 %reduce-scatter.39.cloned.1.call-done = bf16[128,512]{1,0:T(8,128)(2,1)} async-done(((bf16[1024,512]{1,0:T(8,128)(2,1)}), bf16[128,512]{1,0:T(8,128)(2,1)}) %reduce-scatter.39.cloned.1.call-update) | async-done | bytes 131088 | tf_op jit(solution)/shard_map/reduce_scatter | solution.py:167
  2076.7 32.8 %reduce-scatter.37.cloned.1.call-done = bf16[128,512]{1,0:T(8,128)(2,1)} async-done(((bf16[1024,512]{1,0:T(8,128)(2,1)}), bf16[128,512]{1,0:T(8,128)(2,1)}) %reduce-scatter.37.cloned.1.call-update) | async-done | bytes 131088 | tf_op jit(solution)/shard_map/reduce_scatter | solution.py:167
  2111.3 52.1 %reduce-scatter.35.cloned.1.call-done = bf16[512,1024]{1,0:T(8,128)(2,1)} async-done(((bf16[2048,1024]{1,0:T(8,128)(2,1)}), bf16[512,1024]{1,0:T(8,128)(2,1)}) %reduce-scatter.35.cloned.1.call-update) | async-done | bytes 1048592 | tf_op jit(solution)/shard_map/reduce_scatter | solution.py:414
  2165.5 28.7 %all-reduce.36 = (bf16[1024]{0:T(1024)(128)(2,1)S(1)}, bf16[1024]{0:T(1024)(128)(2,1)S(1)}, bf16[2304]{0:T(1024)(128)(2,1)S(1)}, bf16[2304]{0:T(1024)(128)(2,1)S...) all-reduce(bf16[1024]{0:T(1024)(128)(2,1)S(1)} %copy-done.101, ...), channel_id=39, replica_groups=mesh['dp'=4,'ctx'=2,'tensor'=4] {'dp','ctx'}, use_global_device_ids=true, to_apply=%region_82.83.clone | all-reduce | flops 10944 | bytes 43776
  (1740 shorter events, 1592.0 us)
Async XLA Ops:
  7.3 133.9 %all-gather.53.cloned.1.call-start = ((), (), s32[]{:S(2)}) async-start(), calls=%async_computation.30 | async-start | bytes 1179648 | tf_op jit(solution)/shard_map/all_gather | solution.py:148
  9.1 132.1 %all-gather.55.cloned.1.call-start = ((), (), s32[]{:S(2)}) async-start(), calls=%async_computation.31 | async-start | bytes 1179648 | tf_op jit(solution)/shard_map/all_gather | solution.py:149
  10.8 130.4 %all-gather.45.cloned.1.call-start = ((), (), s32[]{:S(2)}) async-start(), calls=%async_computation.16 | async-start | bytes 5242880 | tf_op jit(solution)/shard_map/all_gather | solution.py:234
  30.2 403.2 %all-gather.57.cloned.1.call-start = ((), (), s32[]{:S(2)}) async-start(), calls=%async_computation.32 | async-start | bytes 1179648 | tf_op jit(solution)/shard_map/all_gather | solution.py:158
  31.0 461.6 %reduce-scatter.29.cloned.1.call-start = ((), (), s32[]{:S(2)}) async-start(), calls=%async_computation.17 | async-start | bytes 5242880 | tf_op jit(solution)/shard_map/reduce_scatter | solution.py:280
  440.8 102.4 %all-gather.61.cloned.1.call-start = ((), (), s32[]{:S(2)}) async-start(), calls=%async_computation.34 | async-start | bytes 1179648 | tf_op jit(solution)/shard_map/all_gather | solution.py:149
  441.6 156.6 %all-gather.47.cloned.1.call-start = ((), (), s32[]{:S(2)}) async-start(), calls=%async_computation.18 | async-start | bytes 5242880 | tf_op jit(solution)/shard_map/all_gather | solution.py:234
  497.1 389.3 %all-gather.63.cloned.1.call-start = ((), (), s32[]{:S(2)}) async-start(), calls=%async_computation.35 | async-start | bytes 1179648 | tf_op jit(solution)/shard_map/all_gather | solution.py:158
  497.9 448.6 %reduce-scatter.31.cloned.1.call-start = ((), (), s32[]{:S(2)}) async-start(), calls=%async_computation.19 | async-start | bytes 5242880 | tf_op jit(solution)/shard_map/reduce_scatter | solution.py:280
  893.3 109.1 %all-gather.49.cloned.1.call-start = ((), (), s32[]{:S(2)}) async-start(), calls=%async_computation.20 | async-start | bytes 5242880 | tf_op jit(solution)/shard_map/all_gather | solution.py:353
  949.4 406.7 %reduce-scatter.33.cloned.1.call-start = ((), (), s32[]{:S(2)}) async-start(), calls=%async_computation.21 | async-start | bytes 5242880 | tf_op jit(solution)/shard_map/reduce_scatter | solution.py:414
  1303.3 131.3 %all-gather.51.cloned.1.call-start = ((), (), s32[]{:S(2)}) async-start(), calls=%async_computation.22 | async-start | bytes 5242880 | tf_op jit(solution)/shard_map/all_gather | solution.py:353
  1363.0 380.2 %reduce-scatter.47.cloned.1.call-start = ((), (), s32[]{:S(2)}) async-start(), calls=%async_computation.29 | async-start | bytes 589824 | tf_op jit(solution)/shard_map/reduce_scatter | solution.py:173
  1425.1 318.1 %reduce-scatter.45.cloned.1.call-start = ((), (), s32[]{:S(2)}) async-start(), calls=%async_computation.28 | async-start | bytes 589824 | tf_op jit(solution)/shard_map/reduce_scatter | solution.py:173
  1715.3 122.0 %reduce-scatter.59.cloned.1.call-start = ((), (), s32[]{:S(2)}) async-start(), calls=%async_computation.41 | async-start | bytes 1179648
  1722.7 146.6 %reduce-scatter.53.cloned.1.call-start = ((), (), s32[]{:S(2)}) async-start(), calls=%async_computation.38 | async-start | bytes 663552
  1739.0 160.9 %reduce-scatter.49.cloned.1.call-start = ((), (), s32[]{:S(2)}) async-start(), calls=%async_computation.36 | async-start | bytes 294912
  1743.1 200.3 %all-reduce.42.cloned.1.call-start = ((), (), s32[]{:S(2)}) async-start(), calls=%async_computation.42 | async-start | bytes 262144 | tf_op jit(solution)/shard_map/psum | solution.py:203
  1743.8 234.2 %reduce-scatter.57.cloned.1.call-start = ((), (), s32[]{:S(2)}) async-start(), calls=%async_computation.40 | async-start | bytes 1179648
  1753.2 257.7 %reduce-scatter.43.cloned.1.call-start = ((), (), s32[]{:S(2)}) async-start(), calls=%async_computation.27 | async-start | bytes 1179648 | tf_op jit(solution)/shard_map/reduce_scatter | solution.py:170
  1754.9 288.8 %reduce-scatter.41.cloned.1.call-start = ((), (), s32[]{:S(2)}) async-start(), calls=%async_computation.26 | async-start | bytes 1179648 | tf_op jit(solution)/shard_map/reduce_scatter | solution.py:170
  1758.0 318.7 %reduce-scatter.39.cloned.1.call-start = ((), (), s32[]{:S(2)}) async-start(), calls=%async_computation.25 | async-start | bytes 1179648 | tf_op jit(solution)/shard_map/reduce_scatter | solution.py:167
  1758.7 350.8 %reduce-scatter.37.cloned.1.call-start = ((), (), s32[]{:S(2)}) async-start(), calls=%async_computation.24 | async-start | bytes 1179648 | tf_op jit(solution)/shard_map/reduce_scatter | solution.py:167
  1759.3 404.1 %reduce-scatter.35.cloned.1.call-start = ((), (), s32[]{:S(2)}) async-start(), calls=%async_computation.23 | async-start | bytes 5242880 | tf_op jit(solution)/shard_map/reduce_scatter | solution.py:414
  (171 other events, 6224.5 us)
Sparse Core Ops, SparseCore 0:
  9.7 24.9 all-gather.52
  61.0 52.5 all-gather.44
  115.1 23.9 all-gather.56
  440.3 52.1 reduce-scatter.28
  494.1 25.1 all-gather.58
  545.8 52.3 all-gather.46
  893.4 52.9 reduce-scatter.30
  949.5 52.8 all-gather.48
  1303.4 52.6 reduce-scatter.32
  1363.1 52.7 all-gather.50
  1425.2 30.8 reduce-scatter.46
  1710.3 31.6 reduce-scatter.44
  1744.3 29.2 reduce-scatter.54
  1776.3 28.5 reduce-scatter.50
  1807.1 30.2 reduce-scatter.58
  1839.7 29.5 reduce-scatter.52
  1871.4 28.5 reduce-scatter.48
  1903.1 40.2 all-reduce.41
  1945.6 32.3 reduce-scatter.56
  1980.3 30.5 reduce-scatter.42
  2013.0 30.6 reduce-scatter.40
  2046.0 30.6 reduce-scatter.38
  2078.8 30.6 reduce-scatter.36
  2112.3 51.0 reduce-scatter.34
  (3 shorter events, 67.1 us)
where the time goes:
time: 2250 us; the launch traced here: 2230 us
  matrix products  553 us (25%)
  waiting for transfers between devices  552 us (25%)
  local copies, waits for them, and re-layouts  538 us (24%)
  other arithmetic  277 us (12%)
  blocking collectives  269 us (12%)
    dynamic_update_slice x32, local copies, waits for them, and re-layouts, scan_blocks(): lax.scan(jax.checkpoint(ssd_block), zero_state, pieces)  225 us
    dot_general x48, matrix products, ssd_block(): inside = jnp.einsum('tsh,shp->thp', mixing, head_x, precision=HIGH)  171 us
    unnamed x33, waiting for transfers between devices  155 us
    reduce_scatter x2, waiting for transfers between devices, layer_backward(): lax.psum_scatter(grad_rows_in.astype(jnp.bfloat16), 'tensor', scatter_dim...  104 us
    another operation x176, other arithmetic  98.5 us
    dot_general x64, matrix products, ssd_block(): jnp.einsum('sh,sn,shp->hpn', tail_weight, proj_b, head_x, precision=HIGH)  80.8 us
    unnamed x6, blocking collectives  79.6 us
    dot_general x64, matrix products, ssd_block(): jnp.dot(proj_c, proj_b.T, precision=HIGH, preferred_element_type=jnp.floa...  64.2 us
  transfers between devices with their start and end apart: 31, of which 17 were waited for; matrix products, arithmetic and copies ran while one was open for 47% of the time, Pallas kernels for 0%

commit v1 on v0

v1 whole, which is shorter than its diff:
```python
import jax
import jax.numpy as jnp
from jax import lax
from jax.experimental import pallas as pl
from jax.experimental.pallas import tpu as pltpu
from jax.sharding import PartitionSpec as P

NH = 32
HEADDIM = 64
NSTATE = 128
KCONV = 4
SPAN = 256
LAYERS = 2
INNER = 2048
LANES = 128
SMALL_ROWS = 16

EPS = 1e-05
HIGH = lax.Precision.HIGHEST
BF = jnp.bfloat16
F32 = jnp.float32


def dot(left, right, lc=1, rc=0):
    return lax.dot_general(left, right, (((lc,), (rc,)), ((), ())), preferred_element_type=F32)


def exact(left, right):
    return jnp.dot(left, right, precision=HIGH, preferred_element_type=F32)


def silu_grad(values):
    sigmoid_v = jax.nn.sigmoid(values)
    return sigmoid_v * (1.0 + values * (1.0 - sigmoid_v))


def causal_mask(size):
    rows = lax.broadcasted_iota(jnp.int32, (size, size), 0)
    cols = lax.broadcasted_iota(jnp.int32, (size, size), 1)
    return rows >= cols


def scan_fwd_kernel(b_ref, c_ref, xd_ref, xw_ref, e_ref, a_ref, at_ref, el_ref, y_ref, s_ref, f_ref, state):
    @pl.when(pl.program_id(0) == 0)
    def _():
        state[...] = jnp.zeros_like(state)

    heads = a_ref.shape[1]
    b, c = b_ref[...], c_ref[...]
    held = state[...]
    s_ref[0] = held
    scores = jnp.where(causal_mask(b.shape[0]), dot(c, b, 1, 1), 0.0)
    carried = e_ref[...] * dot(c, held.astype(BF))
    for h in range(heads):
        at = slice(h * HEADDIM, (h + 1) * HEADDIM)
        spread = jnp.minimum(a_ref[:, h : h + 1] - at_ref[0, h : h + 1, :], 0.0)
        mixing = (scores * jnp.exp(spread)).astype(BF)
        y_ref[:, at] = dot(mixing, xd_ref[:, at]) + carried[:, at]
    new = el_ref[0] * held + dot(b, xw_ref[...], 0, 0)
    state[...] = new
    f_ref[...] = new


def scan_bwd_kernel(b_ref, c_ref, xd_ref, xw_ref, dy_ref, z_ref, a_ref, at_ref, el_ref, s_ref, df_ref,
                    dx_ref, v_ref, db_ref, dc_ref, r_ref, state):
    @pl.when(pl.program_id(0) == 0)
    def _():
        state[...] = df_ref[...]

    heads = a_ref.shape[1]
    b, c, xw, z = b_ref[...], c_ref[...], xw_ref[...], z_ref[...]
    held = state[...]
    low = held.astype(BF)
    entered = s_ref[0]
    mask = causal_mask(b.shape[0])
    scores = jnp.where(mask, dot(c, b, 1, 1), 0.0)
    v_ref[...] = dot(b, low)
    r_ref[0] = el_ref[0] * jnp.sum(held * entered, axis=0, keepdims=True)
    total = jnp.zeros(scores.shape, F32)
    for h in range(heads):
        at = slice(h * HEADDIM, (h + 1) * HEADDIM)
        decays = jnp.exp(jnp.minimum(a_ref[:, h : h + 1] - at_ref[0, h : h + 1, :], 0.0))
        mixing = (scores * decays).astype(BF)
        dy = dy_ref[:, at]
        dx_ref[:, at] = dot(mixing, dy, 0, 0)
        total = total + decays * dot(dy, xd_ref[:, at], 1, 1)
    total = jnp.where(mask, total, 0.0).astype(BF)
    dc_ref[...] = dot(total, b) + dot(z, entered.astype(BF), 1, 1)
    db_ref[...] = dot(total, c, 0, 0) + dot(xw, low, 1, 1)
    state[...] = el_ref[0] * held + dot(c, z, 0, 0)


def rows_of(width, order):
    return pl.BlockSpec((SPAN, width), lambda k: (order(k), 0))


def one_of(rows, width, order):
    return pl.BlockSpec((1, rows, width), lambda k: (order(k), 0, 0))


PARAMS = pltpu.CompilerParams(vmem_limit_bytes=48 * 1024 * 1024)


def scan_fwd(b, c, xd, xw, e, a, at, el):
    length, wide = xd.shape
    heads, count = a.shape[1], length // SPAN
    order = lambda k: k
    return pl.pallas_call(
        scan_fwd_kernel,
        grid=(count,),
        in_specs=[
            rows_of(NSTATE, order), rows_of(NSTATE, order), rows_of(wide, order), rows_of(wide, order),
            rows_of(wide, order), rows_of(heads, order), one_of(heads, SPAN, order), one_of(1, wide, order),
        ],
        out_specs=[
            rows_of(wide, order), one_of(NSTATE, wide, order),
            pl.BlockSpec((NSTATE, wide), lambda k: (0, 0)),
        ],
        out_shape=[
            jax.ShapeDtypeStruct((length, wide), F32),
            jax.ShapeDtypeStruct((count, NSTATE, wide), F32),
            jax.ShapeDtypeStruct((NSTATE, wide), F32),
        ],
        scratch_shapes=[pltpu.VMEM((NSTATE, wide), F32)],
        compiler_params=PARAMS,
    )(b, c, xd, xw, e, a, at, el)


def scan_bwd(b, c, xd, xw, dy, z, a, at, el, s, df):
    length, wide = xd.shape
    heads, count = a.shape[1], length // SPAN
    order = lambda k: count - 1 - k
    return pl.pallas_call(
        scan_bwd_kernel,
        grid=(count,),
        in_specs=[
            rows_of(NSTATE, order), rows_of(NSTATE, order), rows_of(wide, order), rows_of(wide, order),
            rows_of(wide, order), rows_of(wide, order), rows_of(heads, order), one_of(heads, SPAN, order),
            one_of(1, wide, order), one_of(NSTATE, wide, order),
            pl.BlockSpec((NSTATE, wide), lambda k: (0, 0)),
        ],
        out_specs=[
            rows_of(wide, order), rows_of(wide, order), rows_of(NSTATE, order), rows_of(NSTATE, order),
            one_of(1, wide, order),
        ],
        out_shape=[
            jax.ShapeDtypeStruct((length, wide), F32),
            jax.ShapeDtypeStruct((length, wide), F32),
            jax.ShapeDtypeStruct((length, NSTATE), F32),
            jax.ShapeDtypeStruct((length, NSTATE), F32),
            jax.ShapeDtypeStruct((count, 1, wide), F32),
        ],
        scratch_shapes=[pltpu.VMEM((NSTATE, wide), F32)],
        compiler_params=PARAMS,
    )(b, c, xd, xw, dy, z, a, at, el, s, df)


def pack_small(pieces, width):
    flat = jnp.concatenate([piece.reshape(-1) for piece in pieces])
    return jnp.pad(flat, (0, SMALL_ROWS * width - flat.shape[0])).reshape(SMALL_ROWS, width)


def fetch_layer(stack, layer):
    gain, w_z, w_x, w_bc, w_dt, conv_w, conv_b, dt_bias, a_log, d_skip, norm_w, w_out = (
        weight[layer] for weight in stack
    )
    rows, inner = w_z.shape
    main = jnp.concatenate([w_z, w_x, w_bc, w_dt, w_out.T], axis=1)
    width = main.shape[1]
    small = (conv_w, conv_b, norm_w, gain, dt_bias, a_log, d_skip)
    full = lax.all_gather(jnp.concatenate([main, pack_small(small, width)], axis=0), ("dp", "ctx"), axis=0)
    peers = full.shape[0]
    wide = full[:, :rows].reshape(peers * rows, width)
    w_main = wide[:, : 2 * inner + 2 * NSTATE]
    at = 2 * inner + 2 * NSTATE
    w_dt_all = wide[:, at : at + NH]
    w_out_t = wide[:, at + NH :]
    flat = full[:, rows:].reshape(peers, -1)
    out, at = [], 0
    for piece in small:
        part = flat[:, at : at + piece.size].reshape((peers,) + piece.shape)
        out.append(jnp.moveaxis(part, 0, -2).reshape(piece.shape[:-1] + (-1,)).astype(F32))
        at += piece.size
    return (w_main, w_dt_all, w_out_t) + tuple(out)


def reduce_layer(parts, peers):
    main, small = parts
    rows = main.shape[0] // peers
    width = main.shape[1]
    flat = jnp.concatenate(
        [
            jnp.moveaxis(p.reshape(p.shape[:-1] + (peers, p.shape[-1] // peers)), -2, 0).reshape(peers, -1)
            for p in small
        ],
        axis=1,
    )
    flat = jnp.pad(flat, ((0, 0), (0, SMALL_ROWS * width - flat.shape[1]))).reshape(peers, SMALL_ROWS, width)
    whole = jnp.concatenate([main.reshape(peers, rows, width), flat.astype(BF)], axis=1)
    return lax.psum_scatter(whole, ("dp", "ctx"), scatter_dimension=0, tiled=False)


def own(vector, start, count):
    return lax.dynamic_slice_in_dim(vector, start, count, vector.ndim - 1)


def place(width, piece, start):
    return lax.dynamic_update_slice_in_dim(
        jnp.zeros(piece.shape[:-1] + (width,), F32), piece, start, piece.ndim - 1
    )


def split_cols(column):
    high = column.astype(BF)
    return high, (column - high.astype(F32)).astype(BF)


def layer_forward(residual, gathered, tensor_at, inner_loc, heads_loc, ctx_at):
    w_main, w_dt, w_out_t, conv_w, conv_b, norm_w, gain, dt_bias, a_log, d_skip = gathered
    head_start = tensor_at * heads_loc
    chan_start = tensor_at * inner_loc
    inv_rms = lax.rsqrt(jnp.mean(residual * residual, axis=-1, keepdims=True) + EPS)
    normed = (residual * inv_rms * gain).astype(BF)
    rows_all = lax.all_gather(normed, "tensor", axis=0, tiled=True)
    length = rows_all.shape[0]
    gate = dot(rows_all, w_main[:, :inner_loc])
    conv_in = dot(rows_all, w_main[:, inner_loc:]).astype(BF)
    w_dt_own = own(w_dt, head_start, heads_loc)
    dt_raw = dot(rows_all, w_dt_own)
    edge = lax.ppermute(conv_in[length - (KCONV - 1) :], "ctx", [(0, 1)])
    conv_w_own = jnp.concatenate([own(conv_w, chan_start, inner_loc), conv_w[:, INNER:]], axis=1)
    conv_b_own = jnp.concatenate([own(conv_b, chan_start, inner_loc), conv_b[INNER:]], axis=0)
    padded = jnp.concatenate([edge, conv_in], axis=0)
    conv_out = conv_b_own + sum(
        conv_w_own[k] * padded[k : k + length].astype(F32) for k in range(KCONV)
    )
    activated = jax.nn.silu(conv_out).astype(BF)
    x = activated[:, :inner_loc]
    b = activated[:, inner_loc : inner_loc + NSTATE]
    c = activated[:, inner_loc + NSTATE :]
    dt_pre = dt_raw + own(dt_bias, head_start, heads_loc)
    delta = jax.nn.softplus(dt_pre)
    rate = -jnp.exp(own(a_log, head_start, heads_loc))
    log_decay = rate * delta
    count = length // SPAN
    spread = jnp.repeat(jnp.eye(heads_loc, dtype=F32), HEADDIM, axis=1)
    lower = causal_mask(SPAN).astype(F32)
    a3 = jnp.einsum("ts,ksh->kth", lower, log_decay.reshape(count, SPAN, heads_loc), precision=HIGH)
    a = a3.reshape(length, heads_loc)
    at = jnp.swapaxes(a3, 1, 2)
    last = a3[:, -1]
    tail = jnp.exp(last[:, None] - a3).reshape(length, heads_loc)
    e_wide = exact(jnp.exp(a), spread)
    delta_wide = exact(delta, spread)
    tail_wide = exact(tail, spread)
    xf = x.astype(F32)
    xd = (xf * delta_wide).astype(BF)
    xw = (xf * (delta_wide * tail_wide)).astype(BF)
    el = exact(jnp.exp(last), spread)[:, None]
    local_y, local_s, final_s = scan_fwd(b, c, xd, xw, e_wide, a, at, el)
    strict = 1.0 - causal_mask(count).astype(F32).T
    before = exact(strict, last)
    first = lax.ppermute(final_s.astype(BF), "ctx", [(0, 1)])
    before_wide = exact(jnp.exp(before), spread)
    e_total = (e_wide.reshape(count, SPAN, -1) * before_wide[:, None]).reshape(length, inner_loc)
    entered = local_s + before_wide[:, None] * first.astype(F32)[None]
    y = local_y + e_total * dot(c, first)
    skip_wide = exact(own(d_skip, head_start, heads_loc)[None], spread)
    scanned = y + skip_wide * xf
    gated = scanned * jax.nn.silu(gate)
    squares = jnp.sum(gated * gated, axis=-1, keepdims=True)
    norm_own = own(norm_w, chan_start, inner_loc)
    branch = (gated * norm_own).astype(BF)
    partial = dot(branch, w_out_t, 1, 1).astype(BF)
    packed = jnp.concatenate(
        [partial, jnp.broadcast_to(squares.astype(BF), (length, LANES))], axis=1
    )
    summed = lax.psum_scatter(packed, "tensor", scatter_dimension=0, tiled=True).astype(F32)
    out_own = summed[:, : partial.shape[1]]
    q = lax.rsqrt(summed[:, partial.shape[1] : partial.shape[1] + 1] / INNER + EPS)
    saved = (
        residual, inv_rms, rows_all, gate, conv_w_own, padded, conv_out, b, c, x, xd, xw, e_wide, e_total,
        delta_wide, tail_wide, a, at, el, entered, y, scanned, gated, branch, out_own, q, w_dt_own,
        skip_wide, norm_own, dt_pre, delta, rate, spread, lower,
    )
    return residual + q * out_own, saved


def layer_backward(grad_own, gathered, saved, tensor_at, inner_loc, heads_loc, ctx_at):
    w_main, w_dt, w_out_t, conv_w, conv_b, norm_w, gain, dt_bias, a_log, d_skip = gathered
    (
        residual, inv_rms, rows_all, gate, conv_w_own, padded, conv_out, b, c, x, xd, xw, e_wide, e_total,
        delta_wide, tail_wide, a, at, el, entered, y, scanned, gated, branch, out_own, q, w_dt_own,
        skip_wide, norm_own, dt_pre, delta, rate, spread, lower,
    ) = saved
    head_start = tensor_at * heads_loc
    chan_start = tensor_at * inner_loc
    length = rows_all.shape[0]
    features = residual.shape[1]
    count = length // SPAN
    dq = jnp.sum(grad_own * out_own, axis=-1, keepdims=True)
    high, rest = split_cols(dq * q * q * q / INNER)
    packed = jnp.concatenate(
        [
            (q * grad_own).astype(BF),
            jnp.broadcast_to(high, (high.shape[0], LANES // 2)),
            jnp.broadcast_to(rest, (high.shape[0], LANES // 2)),
        ],
        axis=1,
    )
    arrived = lax.all_gather(packed, "tensor", axis=0, tiled=True)
    grad_rows = arrived[:, :features]
    scale = (
        arrived[:, features : features + 1].astype(F32)
        + arrived[:, features + LANES // 2 : features + LANES // 2 + 1].astype(F32)
    )
    grad_wout_t = dot(grad_rows, branch, 0, 0)
    grad_branch = dot(grad_rows, w_out_t)
    grad_normw = jnp.sum(grad_branch * gated, axis=0)
    grad_gated = grad_branch * norm_own - scale * gated
    dy = grad_gated * jax.nn.silu(gate)
    grad_gate = grad_gated * scanned * silu_grad(gate)
    xf = x.astype(F32)
    heads = lambda wide: exact(wide, spread.T)
    grad_skip = heads(jnp.sum(dy * xf, axis=0, keepdims=True))[0]
    dy_low = dy.astype(BF)
    z = (e_wide * dy).astype(BF)
    first_grad = dot(c, (e_total * dy).astype(BF), 0, 0)
    final_grad = lax.ppermute(first_grad.astype(BF), "ctx", [(1, 0)]).astype(F32)
    dxp, v, db, dc, carry = scan_bwd(b, c, xd, xw, dy_low, z, a, at, el, entered, final_grad)
    pulled = dxp + tail_wide * v
    grad_x = delta_wide * pulled + skip_wide * dy
    grad_dt = heads(xf * pulled)
    moved = xw.astype(F32) * v
    grad_a = heads(dy_low.astype(F32) * y - xd.astype(F32) * dxp - moved).reshape(count, SPAN, heads_loc)
    ends = heads(carry[:, 0] + jnp.sum(moved.reshape(count, SPAN, inner_loc), axis=1))
    grad_decay = (
        jnp.einsum("ts,kth->ksh", lower, grad_a, precision=HIGH) + ends[:, None]
    ).reshape(length, heads_loc)
    grad_delta = grad_dt + grad_decay * rate
    grad_alog = jnp.sum(grad_decay * delta, axis=0) * rate
    grad_pre = grad_delta * jax.nn.sigmoid(dt_pre)
    grad_dtbias = jnp.sum(grad_pre, axis=0)
    grad_pre_low = grad_pre.astype(BF)
    grad_conv = jnp.concatenate([grad_x, db, dc], axis=1) * silu_grad(conv_out)
    grad_convb = jnp.sum(grad_conv, axis=0)
    grad_convw = jnp.stack(
        [jnp.sum(grad_conv * padded[k : k + length].astype(F32), axis=0) for k in range(KCONV)]
    )
    head_rows = lax.ppermute(grad_conv[: KCONV - 1], "ctx", [(1, 0)])
    extended = jnp.concatenate([grad_conv, head_rows], axis=0)
    grad_convin = sum(
        conv_w_own[k] * extended[KCONV - 1 - k : KCONV - 1 - k + length] for k in range(KCONV)
    )
    grad_proj = jnp.concatenate([grad_gate.astype(BF), grad_convin.astype(BF)], axis=1)
    grad_rows_in = dot(grad_proj, w_main, 1, 1) + dot(grad_pre_low, w_dt_own, 1, 1)
    grad_normed = lax.psum_scatter(
        grad_rows_in.astype(BF), "tensor", scatter_dimension=0, tiled=True
    ).astype(F32)
    grad_wmain = dot(rows_all, grad_proj, 0, 0)
    grad_wdt = place(NH, dot(rows_all, grad_pre_low, 0, 0), head_start)
    unit = residual * inv_rms
    grad_unit = grad_normed * gain
    grad_gain = jnp.sum(grad_normed * unit, axis=0)
    grad_prev = grad_own + inv_rms * (
        grad_unit - unit * jnp.mean(grad_unit * unit, axis=-1, keepdims=True)
    )
    main = jnp.concatenate(
        [grad_wmain.astype(BF), grad_wdt.astype(BF), grad_wout_t.astype(BF)], axis=1
    )
    spread_chan = lambda g: jnp.concatenate(
        [place(INNER, g[..., :inner_loc], chan_start), g[..., inner_loc:]], axis=-1
    )
    small = (
        spread_chan(grad_convw),
        spread_chan(grad_convb),
        place(INNER, grad_normw, chan_start),
        grad_gain,
        place(NH, grad_dtbias, head_start),
        place(NH, grad_alog, head_start),
        place(NH, grad_skip, head_start),
    )
    return grad_prev, (main, small)


def per_device(*arrays):
    tokens, cotangent = arrays[0], arrays[-1]
    stack = arrays[1:-1]
    w_z, conv_w = stack[1], stack[5]
    tensor_at = lax.axis_index("tensor")
    ctx_at = lax.axis_index("ctx")
    groups = lax.axis_size("tensor")
    peers = lax.axis_size("dp") * lax.axis_size("ctx")
    inner_loc, heads_loc = INNER // groups, NH // groups
    residual = tokens[0].astype(F32)
    fetched = [fetch_layer(stack, layer) for layer in range(LAYERS)]
    kept = []
    for layer in range(LAYERS):
        residual, saved = layer_forward(residual, fetched[layer], tensor_at, inner_loc, heads_loc, ctx_at)
        kept.append(saved)
    result = residual.astype(BF)[None]
    grad = cotangent[0].astype(F32)
    reduced = [None] * LAYERS
    for layer in reversed(range(LAYERS)):
        grad, parts = layer_backward(
            grad, fetched[layer], kept[layer], tensor_at, inner_loc, heads_loc, ctx_at
        )
        reduced[layer] = reduce_layer(parts, peers)
    both = jnp.stack(reduced)
    rows = w_z.shape[1]
    at_bc, at_dt = 2 * inner_loc, 2 * inner_loc + 2 * NSTATE
    at_out = at_dt + NH
    shapes = [tuple(stack[i].shape[1:]) for i in (5, 6, 10, 0, 7, 8, 9)]
    sizes = []
    for shape in shapes:
        size = 1
        for extent in shape:
            size *= extent
        sizes.append(size)
    used = sum(sizes)
    mid = both[:, :rows, at_bc:at_out].reshape(LAYERS, -1)
    vec = both[:, rows:].reshape(LAYERS, -1)[:, :used]
    shared = lax.psum(jnp.concatenate([mid, vec], axis=1), "tensor").astype(F32)
    mid_sum = shared[:, : mid.shape[1]].reshape(LAYERS, rows, 2 * NSTATE + NH)
    pieces, at = [], mid.shape[1]
    for shape, size in zip(shapes, sizes):
        pieces.append(shared[:, at : at + size].reshape((LAYERS,) + shape))
        at += size
    g_convw, g_convb, g_normw, g_gain, g_dtb, g_alog, g_skip = pieces
    wide = both[:, :rows].astype(F32)
    return (
        result,
        grad[None],
        g_gain,
        wide[:, :, :inner_loc],
        wide[:, :, inner_loc : 2 * inner_loc],
        mid_sum[:, :, : 2 * NSTATE],
        mid_sum[:, :, 2 * NSTATE :],
        g_convw,
        g_convb,
        g_dtb,
        g_alog,
        g_skip,
        g_normw,
        jnp.swapaxes(wide[:, :, at_out:], 1, 2),
    )


def solution(mesh):
    placed = (
        P("dp", ("ctx", "tensor"), None),
        P(None, ("dp", "ctx")),
        P(None, ("dp", "ctx"), "tensor"),
        P(None, ("dp", "ctx"), "tensor"),
        P(None, ("dp", "ctx"), None),
        P(None, ("dp", "ctx"), None),
        P(None, None, ("dp", "ctx")),
        P(None, ("dp", "ctx")),
        P(None, ("dp", "ctx")),
        P(None, ("dp", "ctx")),
        P(None, ("dp", "ctx")),
        P(None, ("dp", "ctx")),
        P(None, "tensor", ("dp", "ctx")),
        P("dp", ("ctx", "tensor"), None),
    )
    return jax.shard_map(
        per_device,
        mesh=mesh,
        in_specs=placed,
        out_specs=(
            P("dp", ("ctx", "tensor"), None),
            P("dp", ("ctx", "tensor"), None),
            P(None, ("dp", "ctx")),
            P(None, ("dp", "ctx"), "tensor"),
            P(None, ("dp", "ctx"), "tensor"),
            P(None, ("dp", "ctx"), None),
            P(None, ("dp", "ctx"), None),
            P(None, None, ("dp", "ctx")),
            P(None, ("dp", "ctx")),
            P(None, ("dp", "ctx")),
            P(None, ("dp", "ctx")),
            P(None, ("dp", "ctx")),
            P(None, ("dp", "ctx")),
            P(None, "tensor", ("dp", "ctx")),
        ),
        check_vma=False,
    )
```

time: 2250 us -> 1100 us (0.49)
  local copies, waits for them, and re-layouts: 538 us -> 117 us
  matrix products: 553 us -> 185 us
  blocking collectives: 269 us -> 0 us
  other arithmetic: 277 us -> 133 us
  Pallas kernels: 0 us -> 56 us
    dot_general x264 -> x50, matrix products: 553 us -> 185 us  [the longest x24 121 us: dot(): lax.dot_general(left, right, (((lc,), (rc,)), ((), ())), preferred_elemen...]
    dynamic_update_slice x42 -> x12, local copies, waits for them, and re-layouts: 227 us -> 5.71 us  [place(): lax.dynamic_update_slice_in_dim(jnp.zeros(piece.shape[:-1] + (width,), F3...]
    all_gather x18 -> x0, blocking collectives: 173 us -> none  [the longest x2 34.1 us: fetch_layer(): lax.all_gather(pieces[5], ('dp', 'ctx'), axis=1, tiled=True)]
    all_gather x8 -> x4, waiting for transfers between devices: 5.54 us -> 163 us  [the longest x2 112 us: layer_backward(): arrived = lax.all_gather(packed, 'tensor', axis=0, tiled=True)]
    unnamed x33 -> x13, waiting for transfers between devices: 155 us -> 0.21 us
    another operation x190 -> x14, other arithmetic: 109 us -> 0.1 us
    unnamed x6 -> x0, blocking collectives: 79.6 us -> none
    squeeze x64 -> x5, local copies, waits for them, and re-layouts: 63.7 us -> 5.79 us  [fetch_layer(): weight[layer]]
  transfers between devices with their start and end apart: 31 -> 21, of which waited for: 17 -> 16; matrix products, arithmetic and copies ran while one was open for 47% -> 17% of each run, Pallas kernels for 0% -> 1%
where the time goes in v1:
time: 1100 us; the launch traced here: 1090 us
  waiting for transfers between devices  571 us (52%)
  matrix products  185 us (17%)
  other arithmetic  133 us (12%)
  local copies, waits for them, and re-layouts  117 us (11%)
  Pallas kernels  56 us (5%)
  between operations  16.6 us (2%)
  starting transfers between devices  13.9 us (1%)
    dot_general x24, matrix products, dot(): lax.dot_general(left, right, (((lc,), (rc,)), ((), ())), preferred_elemen...  121 us
    all_gather x2, waiting for transfers between devices, layer_backward(): arrived = lax.all_gather(packed, 'tensor', axis=0, tiled=True)  112 us
    reduce_scatter x2, waiting for transfers between devices, layer_forward(): lax.psum_scatter(packed, 'tensor', scatter_dimension=0, tiled=True)  110 us
    reduce_scatter x2, waiting for transfers between devices, reduce_layer(): lax.psum_scatter(whole, ('dp', 'ctx'), scatter_dimension=0, tiled=False)  105 us
    all_gather x2, waiting for transfers between devices, layer_forward(): rows_all = lax.all_gather(normed, 'tensor', axis=0, tiled=True)  85.4 us
    reduce_scatter x2, waiting for transfers between devices, layer_backward(): lax.psum_scatter(grad_rows_in.astype(BF), 'tensor', scatter_dimension=0,...  67.6 us
    dot_general x22, matrix products, exact(): return jnp.dot(left, right, precision=HIGH, preferred_element_type=F32)  62.6 us
    all_gather x2, waiting for transfers between devices, fetch_layer(): lax.all_gather(jnp.concatenate([main, pack_small(small, width)], axis=0),...  51.2 us
  transfers between devices with their start and end apart: 21, of which 16 were waited for; matrix products, arithmetic and copies ran while one was open for 17% of the time, Pallas kernels for 1%

profile of v1, /device:TPU:0, one launch (start us, length us, event | category | flops | bytes accessed | tf_op | source)
XLA Modules:
  0.0 1092.6 jit_solution(2685864984213771551)
XLA Ops:
  20.1 51.2 %all-gather.17.cloned.1.call-done = bf16[1152,1824]{1,0:T(8,128)(2,1)} async-done(((bf16[144,1824]{1,0:T(8,128)(2,1)}), bf16[1152,1824]{1,0:T(8,128)(2,1)}) %all-gather.17.cloned.1.call-update) | async-done | bytes 4202512 | tf_op jit(solution)/shard_map/all_gather | solution.py:171
  85.2 40.6 %all-gather.9.cloned.1.call-done = bf16[2048,1024]{0,1:T(8,128)(2,1)} async-done(((bf16[512,1024]{0,1:T(8,128)(2,1)}), bf16[2048,1024]{0,1:T(8,128)(2,1)}) %all-gather.9.cloned.1.call-update) | async-done | bytes 4194320 | tf_op jit(solution)/shard_map/all_gather | solution.py:224
  146.5 8.9 multiply_convert_fusion.1
  161.8 11.3 %shard_map.245 = (f32[2048,512]{1,0:T(8,128)}, f32[8,128,512]{2,1,0:T(8,128)S(1)}, f32[128,512]{1,0:T(8,128)S(1)}) custom-call(bf16[2048,128]{1,0:T(8,128)(2,1)S(1)} %get-tuple-element.159.b_ref, bf16[2048,128]{1,0:T(8,128)(2,1)S(1)} %get-tuple-element.158.c_ref, bf16[2048,512]{1,0:T(8,128)(2,1)} %get-tuple-element.153.xd_ref, ...), custom_call_target="tpu_custom_call" | custom-call | tf_op jit(solution)/shard_map/pallas_call | solution.py:108
  193.6 55.5 %reduce-scatter.7.cloned.1.call-done = bf16[512,1152]{0,1:T(8,128)(2,1)} async-done(((bf16[2048,1152]{0,1:T(8,128)(2,1)}), bf16[512,1152]{0,1:T(8,128)(2,1)}) %reduce-scatter.7.cloned.1.call-update) | async-done | bytes 1179664 | tf_op jit(solution)/shard_map/reduce_scatter | solution.py:278
  262.7 44.8 %all-gather.11.cloned.1.call-done = bf16[2048,1024]{0,1:T(8,128)(2,1)} async-done(((bf16[512,1024]{0,1:T(8,128)(2,1)}), bf16[2048,1024]{0,1:T(8,128)(2,1)}) %all-gather.11.cloned.1.call-update) | async-done | bytes 4194320 | tf_op jit(solution)/shard_map/all_gather | solution.py:224
  331.1 9.3 multiply_convert_fusion
  346.9 11.3 %shard_map.246 = (f32[2048,512]{1,0:T(8,128)}, f32[8,128,512]{2,1,0:T(8,128)S(1)}, f32[128,512]{1,0:T(8,128)S(1)}) custom-call(bf16[2048,128]{1,0:T(8,128)(2,1)S(1)} %get-tuple-element.157.b_ref, bf16[2048,128]{1,0:T(8,128)(2,1)S(1)} %get-tuple-element.156.c_ref, bf16[2048,512]{1,0:T(8,128)(2,1)} %get-tuple-element.151.xd_ref, ...), custom_call_target="tpu_custom_call" | custom-call | tf_op jit(solution)/shard_map/pallas_call | solution.py:108
  379.1 54.9 %reduce-scatter.9.cloned.1.call-done = bf16[512,1152]{0,1:T(8,128)(2,1)} async-done(((bf16[2048,1152]{0,1:T(8,128)(2,1)}), bf16[512,1152]{0,1:T(8,128)(2,1)}) %reduce-scatter.9.cloned.1.call-update) | async-done | bytes 1179664 | tf_op jit(solution)/shard_map/reduce_scatter | solution.py:278
  441.3 54.7 %all-gather.13.cloned.1.call-done = bf16[2048,1152]{0,1:T(8,128)(2,1)} async-done(((bf16[512,1152]{0,1:T(8,128)(2,1)}), bf16[2048,1152]{0,1:T(8,128)(2,1)}) %all-gather.13.cloned.1.call-update) | async-done | bytes 4718608 | tf_op jit(solution)/shard_map/all_gather | solution.py:311
  496.8 12.4 %fusion.43 = (f32[512]{0:T(512)}, f32[2048,512]{1,0:T(8,128)S(1)}, bf16[2048,512]{1,0:T(8,128)(2,1)}, f32[512]{0:T(512)}) fusion(bf16[2048,768]{1,0:T(8,128)(2,1)} %copy-done.32, f32[2048,512]{1,0:T(8,128)} %get-tuple-element.204, f32[2048,512]{1,0:T(8,128)} %copy-done.144, f32[2048]{0:T(1024)S(1)} %bitcast.279, f32[512]{0:T(512)} %dynamic_slice.55, ...), kind=kOutput, calls=%fused_computation.93 | convolution fusion | flops 2170551296 | bytes 26230784 | tf_op jit(solution)/shard_map/dot_general | solution.py:25
  517.5 16.7 %shard_map.247 = (f32[2048,512]{1,0:T(8,128)}, f32[2048,512]{1,0:T(8,128)}, f32[2048,128]{1,0:T(8,128)S(1)}, f32[2048,128]{1,0:T(8,128)S(1)}, f32[8,1,512]{2,1,0:T(1,128)S(1)}) custom-call(bf16[2048,128]{1,0:T(8,128)(2,1)S(1)} %get-tuple-element.157.b_ref, bf16[2048,128]{1,0:T(8,128)(2,1)S(1)} %get-tuple-element.156.c_ref, ...), custom_call_target="tpu_custom_call" | custom-call | tf_op jit(solution)/shard_map/pallas_call | solution.py:133
  538.3 11.9 %multiply_add_fusion.2 = (f32[2048,512]{1,0:T(8,128)}, f32[2048,512]{1,0:T(8,128)}) fusion(f32[2048,512]{1,0:T(8,128)} %copy-done.45, f32[2048,512]{1,0:T(8,128)} %get-tuple-element.203, f32[512]{0:T(512)S(1)} %bitcast.276, f32[2048,512]{1,0:T(8,128)} %get-tuple-element.35, f32[2048,512]{1,0:T(8,128)S(1)} %copy-done.15, f32[2048,512]{1,0:T(8,128)} %get-tuple-element.36, ...), kind=kLoop, calls=%fused_computation.110 | loop fusion | flops 13631488 | bytes 39847936 | tf_op jit(solution)/shard_map/add | solution.py:332
  588.7 53.5 %reduce-scatter.11.cloned.1.call-done = bf16[512,1024]{0,1:T(8,128)(2,1)} async-done(((bf16[2048,1024]{0,1:T(8,128)(2,1)}), bf16[512,1024]{0,1:T(8,128)(2,1)}) %reduce-scatter.11.cloned.1.call-update) | async-done | bytes 1048592 | tf_op jit(solution)/shard_map/reduce_scatter | solution.py:357
  652.0 57.0 %all-gather.15.cloned.1.call-done = bf16[2048,1152]{0,1:T(8,128)(2,1)} async-done(((bf16[512,1152]{0,1:T(8,128)(2,1)}), bf16[2048,1152]{0,1:T(8,128)(2,1)}) %all-gather.15.cloned.1.call-update) | async-done | bytes 4718608 | tf_op jit(solution)/shard_map/all_gather | solution.py:311
  709.7 12.0 %fusion.38 = (f32[512]{0:T(512)}, f32[2048,512]{1,0:T(8,128)S(1)}, bf16[2048,512]{1,0:T(8,128)(2,1)}, f32[512]{0:T(512)}) fusion(bf16[2048,768]{1,0:T(8,128)(2,1)} %copy-done.30, f32[2048,512]{1,0:T(8,128)} %get-tuple-element.200, f32[2048,512]{1,0:T(8,128)} %copy-done.143, f32[2048]{0:T(1024)S(1)} %bitcast.280, f32[512]{0:T(512)S(1)} %copy-done.130, ...), kind=kOutput, calls=%fused_computation.88 | convolution fusion | flops 2170551296 | bytes 26230784 | tf_op jit(solution)/shard_map/dot_general | solution.py:25
  732.1 16.7 %shard_map.248 = (f32[2048,512]{1,0:T(8,128)}, f32[2048,512]{1,0:T(8,128)}, f32[2048,128]{1,0:T(8,128)S(1)}, f32[2048,128]{1,0:T(8,128)S(1)}, f32[8,1,512]{2,1,0:T(1,128)S(1)}) custom-call(bf16[2048,128]{1,0:T(8,128)(2,1)S(1)} %copy-done.3, bf16[2048,128]{1,0:T(8,128)(2,1)S(1)} %copy-done.1, bf16[2048,512]{1,0:T(8,128)(2,1)} %get-tuple-element.153.xd_ref, ...), custom_call_target="tpu_custom_call" | custom-call | tf_op jit(solution)/shard_map/pallas_call | solution.py:133
  752.9 12.0 %multiply_add_fusion = (f32[2048,512]{1,0:T(8,128)}, f32[2048,512]{1,0:T(8,128)}) fusion(f32[2048,512]{1,0:T(8,128)} %copy-done.46, f32[2048,512]{1,0:T(8,128)} %get-tuple-element.199, f32[512]{0:T(512)S(1)} %bitcast.273, f32[2048,512]{1,0:T(8,128)} %get-tuple-element.41, f32[2048,512]{1,0:T(8,128)S(1)} %copy-done.13, f32[2048,512]{1,0:T(8,128)} %get-tuple-element.42, ...), kind=kLoop, calls=%fused_computation.102 | loop fusion | flops 13631488 | bytes 39847936 | tf_op jit(solution)/shard_map/add | solution.py:332
  817.2 9.1 convolution_convert_fusion.1
  839.5 14.0 %reduce-scatter.13.cloned.1.call-done = bf16[512,1024]{0,1:T(8,128)(2,1)} async-done(((bf16[2048,1024]{0,1:T(8,128)(2,1)}), bf16[512,1024]{0,1:T(8,128)(2,1)}) %reduce-scatter.13.cloned.1.call-update) | async-done | bytes 1048592 | tf_op jit(solution)/shard_map/reduce_scatter | solution.py:357
  880.6 10.1 convolution_convert_fusion
  923.8 24.6 %reduce-scatter.15.cloned.1.call-done = bf16[1,144,1824]{1,2,0:T(8,128)(2,1)} async-done(((bf16[8,144,1824]{1,2,0:T(8,128)(2,1)}), bf16[1,144,1824]{1,2,0:T(8,128)(2,1)}) %reduce-scatter.15.cloned.1.call-update) | async-done | bytes 525328 | tf_op jit(solution)/shard_map/reduce_scatter | solution.py:200
  949.7 80.3 %reduce-scatter.17.cloned.1.call-done = bf16[1,144,1824]{1,2,0:T(8,128)(2,1)} async-done(((bf16[8,144,1824]{1,2,0:T(8,128)(2,1)}), bf16[1,144,1824]{1,2,0:T(8,128)(2,1)}) %reduce-scatter.17.cloned.1.call-update) | async-done | bytes 525328 | tf_op jit(solution)/shard_map/reduce_scatter | solution.py:200
  1038.7 37.8 %all-reduce.6.cloned.1.call-done = bf16[2,38700]{1,0:T(2,128)(2,1)} async-done(((bf16[2,38700]{1,0:T(2,128)(2,1)}), bf16[2,38700]{1,0:T(2,128)(2,1)}) %all-reduce.6.cloned.1.call-update) | async-done | bytes 154816 | tf_op jit(solution)/shard_map/psum | solution.py:423
  (649 shorter events, 365.3 us)
Async XLA Ops:
  7.2 64.1 %all-gather.17.cloned.1.call-start = ((), (), s32[]{:S(2)}) async-start(), calls=%async_computation.17 | async-start | bytes 4976640 | tf_op jit(solution)/shard_map/all_gather | solution.py:171
  19.2 106.6 %all-gather.9.cloned.1.call-start = ((), (), s32[]{:S(2)}) async-start(), calls=%async_computation.6 | async-start | bytes 5242880 | tf_op jit(solution)/shard_map/all_gather | solution.py:224
  19.8 230.9 %copy-start.24 = (bf16[1,512,1024]{1,2,0:T(8,128)(2,1)}, bf16[1,512,1024]{1,2,0:T(8,128)(2,1)S(1)}, u32[]{:S(2)}) copy-start(bf16[1,512,1024]{1,2,0:T(8,128)(2,1)S(1)} %copy.84) | copy-start | bytes 3145732
  74.2 117.6 %all-gather.19.cloned.1.call-start = ((), (), s32[]{:S(2)}) async-start(), calls=%async_computation.18 | async-start | bytes 4976640 | tf_op jit(solution)/shard_map/all_gather | solution.py:171
  77.9 171.1 %reduce-scatter.7.cloned.1.call-start = ((), (), s32[]{:S(2)}) async-start(), calls=%async_computation.7 | async-start | bytes 5898240 | tf_op jit(solution)/shard_map/reduce_scatter | solution.py:278
  84.9 101.9 %copy-start.129 = (f32[512]{0:T(512)}, f32[512]{0:T(512)S(1)}, u32[]{:S(2)}) copy-start(f32[512]{0:T(512)S(1)} %dynamic_slice.48) | copy-start | bytes 6148
  85.1 93.5 %copy-start.116 = (f32[1,512]{1,0:T(1,128)}, f32[1,512]{1,0:T(1,128)S(1)}, u32[]{:S(2)}) copy-start(f32[1,512]{1,0:T(1,128)S(1)} %fusion.166) | copy-start | bytes 6148
  132.2 14.2 %collective-permute-start = (bf16[3,768]{1,0:T(4,128)(2,1)S(1)}, bf16[3,768]{1,0:T(4,128)(2,1)S(1)}, u32[]{:S(2)}, u32[]{:S(2)}) collective-permute-start(bf16[3,768]{1,0:T(4,128)(2,1)S(1)} %slice.524), channel_id=1, source_target_pairs={{0,4},{1,5},{2,6},{3,7},{8,12},{9,13},{10,14},{11,15},{16,20},{17,... | collective-permute-start | bytes 13832 | tf_op jit(solution)/shard_map/ppermute | solution.py:230
  173.2 2.3 collective-permute-start.1
  191.8 115.7 %all-gather.11.cloned.1.call-start = ((), (), s32[]{:S(2)}) async-start(), calls=%async_computation.8 | async-start | bytes 5242880 | tf_op jit(solution)/shard_map/all_gather | solution.py:224
  254.7 179.3 %reduce-scatter.9.cloned.1.call-start = ((), (), s32[]{:S(2)}) async-start(), calls=%async_computation.9 | async-start | bytes 5898240 | tf_op jit(solution)/shard_map/reduce_scatter | solution.py:278
  317.1 13.4 %collective-permute-start.2 = (bf16[3,768]{1,0:T(4,128)(2,1)S(1)}, bf16[3,768]{1,0:T(4,128)(2,1)S(1)}, u32[]{:S(2)}, u32[]{:S(2)}) collective-permute-start(bf16[3,768]{1,0:T(4,128)(2,1)S(1)} %slice.556), channel_id=1, source_target_pairs={{0,4},{1,5},{2,6},{3,7},{8,12},{9,13},{10,14},{11,15},{16,20},{17,... | collective-permute-start | bytes 13832 | tf_op jit(solution)/shard_map/ppermute | solution.py:230
  358.2 2.3 collective-permute-start.3
  376.8 119.2 %all-gather.13.cloned.1.call-start = ((), (), s32[]{:S(2)}) async-start(), calls=%async_computation.10 | async-start | bytes 5898240 | tf_op jit(solution)/shard_map/all_gather | solution.py:311
  438.9 203.4 %reduce-scatter.11.cloned.1.call-start = ((), (), s32[]{:S(2)}) async-start(), calls=%async_computation.11 | async-start | bytes 5242880 | tf_op jit(solution)/shard_map/reduce_scatter | solution.py:357
  514.2 3.2 collective-permute-start.4
  573.3 3.1 collective-permute-start.5
  588.7 120.2 %all-gather.15.cloned.1.call-start = ((), (), s32[]{:S(2)}) async-start(), calls=%async_computation.12 | async-start | bytes 5898240 | tf_op jit(solution)/shard_map/all_gather | solution.py:311
  651.9 201.6 %reduce-scatter.13.cloned.1.call-start = ((), (), s32[]{:S(2)}) async-start(), calls=%async_computation.13 | async-start | bytes 5242880 | tf_op jit(solution)/shard_map/reduce_scatter | solution.py:357
  728.7 3.2 collective-permute-start.6
  786.3 3.1 collective-permute-start.7
  800.1 148.3 %reduce-scatter.15.cloned.1.call-start = ((), (), s32[]{:S(2)}) async-start(), calls=%async_computation.14 | async-start | bytes 8404992 | tf_op jit(solution)/shard_map/reduce_scatter | solution.py:200
  867.3 162.7 %reduce-scatter.17.cloned.1.call-start = ((), (), s32[]{:S(2)}) async-start(), calls=%async_computation.15 | async-start | bytes 8404992 | tf_op jit(solution)/shard_map/reduce_scatter | solution.py:200
  915.3 161.2 %all-reduce.6.cloned.1.call-start = ((), (), s32[]{:S(2)}) async-start(), calls=%async_computation.16 | async-start | bytes 310272 | tf_op jit(solution)/shard_map/psum | solution.py:423
  (144 other events, 2417.9 us)
Sparse Core Ops, SparseCore 0:
  19.3 51.9 all-gather.16
  74.4 51.3 all-gather.8
  127.4 49.2 all-gather.18
  191.9 57.0 reduce-scatter.6
  254.8 52.6 all-gather.10
  376.9 57.0 reduce-scatter.8
  439.0 56.9 all-gather.12
  588.8 53.4 reduce-scatter.10
  652.0 56.8 all-gather.14
  800.2 53.2 reduce-scatter.12
  867.4 80.9 reduce-scatter.14
  950.7 79.2 reduce-scatter.16
  1035.9 40.5 all-reduce.5
